TPU v7x, 512 devices: a whole 4x8x8 slice. The times are simulated.
512 devices in a mesh: expert: 64 (over x, z, core), tensor: 8 (over y).
Axes of the slice: x: 4, y: 8, z: 8, core: 2. Of those that a mesh axis runs over, the one named last changes fastest.
Arguments:
- tokens: bfloat16 [8192, 2048], P('expert', 'tensor'), may hold values from -6 to 6
- cotangent: bfloat16 [8192, 2048], P('expert', 'tensor'), may hold values from -6 to 6
- route_ids: int32 [8192, 6], P('expert'), may hold values from 0 to 63, all different within a row
- route_weights: float32 [8192, 6], P('expert'), may hold values from 0.05 to 0.5
- shared_gate: bfloat16 [1408, 2048], P('tensor'), may hold values from -0.125 to 0.125
- shared_up: bfloat16 [1408, 2048], P('tensor'), may hold values from -0.125 to 0.125
- shared_down: bfloat16 [1408, 2048], P('tensor'), may hold values from -0.15625 to 0.15625
- expert_gate: bfloat16 [64, 1408, 2048], P('expert', 'tensor'), may hold values from -0.125 to 0.125
- expert_up: bfloat16 [64, 1408, 2048], P('expert', 'tensor'), may hold values from -0.125 to 0.125
- expert_down: bfloat16 [64, 1408, 2048], P('expert', 'tensor'), may hold values from -0.15625 to 0.15625
Outputs:
- layer_output: bfloat16 [8192, 2048], P('expert', 'tensor')
- input_grad: bfloat16 [8192, 2048], P('expert', 'tensor')
Inputs may be any that keep to these rules, and one draw needn't show every extreme that they name: `route_ids`: each row names 6 different experts.
All inputs are finite; a program needn't handle non-finite values.
Results may differ from a plain program's by a relative error of at most 0.0051.
Values may be sent and summed in bfloat16 or wider, within the bound.
A program may use at most 64 MiB of HBM per device.

v0:
```python
import jax
import jax.numpy as jnp
from jax import lax
from jax.sharding import PartitionSpec as P


def silu_parts(pre_act):
    sigmoid_value = jax.nn.sigmoid(pre_act)
    return (pre_act * sigmoid_value, sigmoid_value * (1.0 + pre_act * (1.0 - sigmoid_value)))


def on_device(
    tokens,
    cotangent,
    route_ids,
    route_weights,
    shared_gate,
    shared_up,
    shared_down,
    expert_gate,
    expert_up,
    expert_down,
):
    expert_count = lax.axis_size("expert")
    tok_rows, top_count = route_ids.shape
    local_experts = expert_gate.shape[0]
    all_experts = local_experts * expert_count
    capacity = tok_rows * top_count // (2 * all_experts)
    slot_total = all_experts * capacity
    flat_ids = route_ids.reshape(-1)
    one_hot = (flat_ids[:, None] == jnp.arange(all_experts, dtype=jnp.int32)[None, :]).astype(
        jnp.int32
    )
    rank_in = jnp.sum((jnp.cumsum(one_hot, axis=0) - one_hot) * one_hot, axis=1)
    kept_mask = rank_in < capacity
    slot_index = jnp.where(kept_mask, flat_ids * capacity + rank_in, slot_total)
    slot_match = jnp.arange(slot_total, dtype=jnp.int32)[:, None] == slot_index[None, :]
    dispatch = jnp.any(slot_match.reshape(slot_total, tok_rows, top_count), axis=2).astype(
        jnp.bfloat16
    )
    gate_flat = route_weights.reshape(-1)
    slot_gate = jnp.sum(jnp.where(slot_match, gate_flat[None, :], 0.0), axis=1)
    gate_dispatch = dispatch.astype(jnp.float32) * slot_gate[:, None]
    x_full, c_full = (
        lax.all_gather(tokens, "tensor", axis=1, tiled=True),
        lax.all_gather(cotangent, "tensor", axis=1, tiled=True),
    )
    x_slots = jnp.dot(dispatch, x_full, preferred_element_type=jnp.float32).astype(jnp.bfloat16)
    g_slots = (
        slot_gate[:, None] * jnp.dot(dispatch, c_full, preferred_element_type=jnp.float32)
    ).astype(jnp.bfloat16)
    x_recv, g_recv = (
        lax.all_to_all(x_slots, "expert", split_axis=0, concat_axis=0, tiled=True),
        lax.all_to_all(g_slots, "expert", split_axis=0, concat_axis=0, tiled=True),
    )

    def owner_layout(values):
        shaped = values.reshape(expert_count, local_experts, capacity, values.shape[-1])
        return shaped.transpose(1, 0, 2, 3).reshape(
            local_experts, expert_count * capacity, values.shape[-1]
        )

    def source_layout(values):
        shaped = values.reshape(local_experts, expert_count, capacity, values.shape[-1])
        return shaped.transpose(1, 0, 2, 3).reshape(slot_total, values.shape[-1])

    x_own = owner_layout(x_recv)
    g_own = owner_layout(g_recv)
    gate_pre = jnp.einsum("erd,efd->erf", x_own, expert_gate, preferred_element_type=jnp.float32)
    up_pre = jnp.einsum("erd,efd->erf", x_own, expert_up, preferred_element_type=jnp.float32)
    act_value, act_slope = silu_parts(gate_pre)
    hidden = (act_value * up_pre).astype(jnp.bfloat16)
    grad_hidden = jnp.einsum("erd,efd->erf", g_own, expert_down, preferred_element_type=jnp.float32)
    grad_gate = (grad_hidden * up_pre * act_slope).astype(jnp.bfloat16)
    grad_up = (grad_hidden * act_value).astype(jnp.bfloat16)
    value_part = source_layout(
        jnp.einsum("erf,efd->erd", hidden, expert_down, preferred_element_type=jnp.float32).astype(
            jnp.bfloat16
        )
    )
    grads_joined = jnp.concatenate((grad_gate, grad_up), axis=2)
    weights_joined = jnp.concatenate((expert_gate, expert_up), axis=1)
    input_term = jnp.einsum(
        "erf,efd->erd", grads_joined, weights_joined, preferred_element_type=jnp.float32
    )
    input_part = source_layout(input_term.astype(jnp.bfloat16))
    shared_gate_pre = jnp.einsum(
        "td,fd->tf", x_full, shared_gate, preferred_element_type=jnp.float32
    )
    shared_up_pre = jnp.einsum("td,fd->tf", x_full, shared_up, preferred_element_type=jnp.float32)
    shared_act, shared_slope = silu_parts(shared_gate_pre)
    shared_hidden = (shared_act * shared_up_pre).astype(jnp.bfloat16)
    shared_value = jnp.dot(shared_hidden, shared_down, preferred_element_type=jnp.float32)
    shared_grad_hidden = jnp.einsum(
        "td,fd->tf", c_full, shared_down, preferred_element_type=jnp.float32
    )
    shared_grad_gate = (shared_grad_hidden * shared_up_pre * shared_slope).astype(jnp.bfloat16)
    shared_grad_up = (shared_grad_hidden * shared_act).astype(jnp.bfloat16)
    shared_input = jnp.dot(shared_grad_gate, shared_gate, preferred_element_type=jnp.float32)
    shared_input = shared_input + jnp.dot(
        shared_grad_up, shared_up, preferred_element_type=jnp.float32
    )
    value_back, input_back = (
        lax.all_to_all(value_part, "expert", split_axis=0, concat_axis=0, tiled=True),
        lax.all_to_all(input_part, "expert", split_axis=0, concat_axis=0, tiled=True),
    )
    early_value = shared_value + jnp.einsum(
        "st,sd->td",
        gate_dispatch,
        value_back.astype(jnp.float32),
        precision=lax.Precision.HIGHEST,
        preferred_element_type=jnp.float32,
    )
    early_input = shared_input + jnp.einsum(
        "st,sd->td",
        dispatch,
        input_back,
        precision=lax.Precision.HIGHEST,
        preferred_element_type=jnp.float32,
    )
    value_total, input_total = (
        lax.psum_scatter(early_value, "tensor", scatter_dimension=1, tiled=True),
        lax.psum_scatter(early_input, "tensor", scatter_dimension=1, tiled=True),
    )
    return (value_total.astype(jnp.bfloat16), input_total.astype(jnp.bfloat16))


def solution(mesh):
    in_specs = (
        P("expert", "tensor"),
        P("expert", "tensor"),
        P("expert", None),
        P("expert", None),
        P("tensor", None),
        P("tensor", None),
        P("tensor", None),
        P("expert", "tensor", None),
        P("expert", "tensor", None),
        P("expert", "tensor", None),
    )
    out_specs = (P("expert", "tensor"), P("expert", "tensor"))
    return jax.shard_map(
        on_device, mesh=mesh, in_specs=in_specs, out_specs=out_specs, check_vma=False
    )
```

profile of v0, /device:TPU:2, one launch (start us, length us, event | category | flops | bytes accessed | tf_op | source)
XLA Modules:
  0.0 333.4 jit_solution(1822526318146382311)
XLA Ops:
  9.0 27.1 %all_gather.6 = bf16[128,2048]{1,0:T(8,128)(2,1)S(1)} all-gather(bf16[128,256]{1,0:T(8,128)(2,1)} %param.10), channel_id=1, replica_groups=mesh['expert'=64,'tensor'=8] {'tensor'}, dimensions={1}, use_global_device_ids=true | all-gather | bytes 589824 | tf_op jit(solution)/shard_map/all_gather | solution.py:45
  36.3 1.8 reduce-window.6
  39.5 1.6 all_to_all.32
  41.1 14.0 %all-to-all-start = ((bf16[64,6,2048]{2,1,0:T(8,128)(2,1)}), bf16[64,6,2048]{2,1,0:T(8,128)(2,1)S(1)}, u32[]{:S(2)}, u32[]{:S(2)}) async-start(bf16[64,6,2048]{2,1,0:T(8,128)(2,1)} %all_to_all.32), calls=%async_computation | async-start | bytes 4194304 | tf_op jit(solution)/shard_map/all_to_all | solution.py:53
  55.6 25.5 %all_gather.7 = bf16[128,2048]{1,0:T(8,128)(2,1)S(1)} all-gather(bf16[128,256]{1,0:T(8,128)(2,1)S(1)} %copy-done.14), channel_id=1, replica_groups=mesh['expert'=64,'tensor'=8] {'tensor'}, dimensions={1}, use_global_device_ids=true | all-gather | bytes 589824 | tf_op jit(solution)/shard_map/all_gather | solution.py:46
  81.9 1.7 multiply_convert_fusion
  83.6 3.7 %all_to_all.38 = bf16[64,6,2048]{2,1,0:T(8,128)(2,1)} reshape(bf16[384,2048]{1,0:T(8,128)(2,1)} %multiply_convert_fusion) | data formatting | bytes 3145728 | tf_op jit(solution)/shard_map/all_to_all | solution.py:54
  87.3 17.3 %all-to-all-done = bf16[64,6,2048]{2,1,0:T(8,128)(2,1)S(1)} async-done(((bf16[64,6,2048]{2,1,0:T(8,128)(2,1)}), bf16[64,6,2048]{2,1,0:T(8,128)(2,1)S(1)}, u32[]{:S(2)}, u32[]{:S(2)}) %all-to-all-start) | async-done | bytes 1572896 | tf_op jit(solution)/shard_map/all_to_all | solution.py:53
  105.9 7.7 %all-to-all-start.2 = ((bf16[64,6,2048]{2,1,0:T(8,128)(2,1)}), bf16[64,6,2048]{2,1,0:T(8,128)(2,1)}, u32[]{:S(2)}, u32[]{:S(2)}) async-start(bf16[64,6,2048]{2,1,0:T(8,128)(2,1)} %all_to_all.38), calls=%async_computation.3 | async-start | bytes 4194304 | tf_op jit(solution)/shard_map/all_to_all | solution.py:54
  113.6 2.6 all_to_all.34
  116.3 1.8 fusion.6
  120.2 1.6 all_to_all.35
  121.7 41.4 %all-to-all-done.2 = bf16[64,6,2048]{2,1,0:T(8,128)(2,1)} async-done(((bf16[64,6,2048]{2,1,0:T(8,128)(2,1)}), bf16[64,6,2048]{2,1,0:T(8,128)(2,1)}, u32[]{:S(2)}, u32[]{:S(2)}) %all-to-all-start.2) | async-done | bytes 1572896 | tf_op jit(solution)/shard_map/all_to_all | solution.py:54
  163.1 7.5 %all-to-all-start.1 = ((bf16[64,6,2048]{2,1,0:T(8,128)(2,1)}), bf16[64,6,2048]{2,1,0:T(8,128)(2,1)S(1)}, u32[]{:S(2)}, u32[]{:S(2)}) async-start(bf16[64,6,2048]{2,1,0:T(8,128)(2,1)} %all_to_all.35), calls=%async_computation.1 | async-start | bytes 4194304 | tf_op jit(solution)/shard_map/all_to_all | solution.py:104
  170.6 3.7 %all_to_all.40 = bf16[384,2048]{1,0:T(8,128)(2,1)} reshape(bf16[64,6,2048]{2,1,0:T(8,128)(2,1)} %all-to-all-done.2) | data formatting | bytes 3145728 | tf_op jit(solution)/shard_map/all_to_all | solution.py:54
  174.4 2.3 fusion.20
  176.7 2.2 convolution_convert_fusion.1
  178.9 3.7 %all_to_all.41 = bf16[64,6,2048]{2,1,0:T(8,128)(2,1)} reshape(bf16[384,2048]{1,0:T(8,128)(2,1)} %convolution_convert_fusion.1) | data formatting | bytes 3145728 | tf_op jit(solution)/shard_map/all_to_all | solution.py:105
  182.5 37.6 %all-to-all-done.1 = bf16[64,6,2048]{2,1,0:T(8,128)(2,1)S(1)} async-done(((bf16[64,6,2048]{2,1,0:T(8,128)(2,1)}), bf16[64,6,2048]{2,1,0:T(8,128)(2,1)S(1)}, u32[]{:S(2)}, u32[]{:S(2)}) %all-to-all-start.1) | async-done | bytes 1572896 | tf_op jit(solution)/shard_map/all_to_all | solution.py:104
  221.5 7.5 %all-to-all-start.3 = ((bf16[64,6,2048]{2,1,0:T(8,128)(2,1)}), bf16[64,6,2048]{2,1,0:T(8,128)(2,1)S(1)}, u32[]{:S(2)}, u32[]{:S(2)}) async-start(bf16[64,6,2048]{2,1,0:T(8,128)(2,1)} %all_to_all.41), calls=%async_computation.4 | async-start | bytes 4194304 | tf_op jit(solution)/shard_map/all_to_all | solution.py:105
  229.3 1.5 fusion.38
  230.8 1.5 fusion.37
  232.3 1.4 fusion.25
  233.7 3.7 %all_to_all.37 = bf16[384,2048]{1,0:T(8,128)(2,1)} reshape(bf16[64,6,2048]{2,1,0:T(8,128)(2,1)} %copy-done.1) | data formatting | bytes 3145728 | tf_op jit(solution)/shard_map/all_to_all | solution.py:104
  237.4 3.9 %convolution_add_fusion.2 = f32[128,2048]{1,0:T(8,128)} fusion(f32[128,2048]{1,0:T(8,128)} %fusion.25, bf16[384,2048]{1,0:T(8,128)(2,1)} %all_to_all.37, f32[384]{0:T(512)S(1)} %select_reduce_fusion, pred[384,128]{1,0:T(8,128)(4,1)S(1)} %fusion.2), kind=kOutput, calls=%fused_computation.6 | convolution fusion | flops 1208369152 | bytes 3720704 | tf_op jit(solution)/shard_map/st,sd->td/dot_general | solution.py:107
  241.4 1.6 fusion.39
  245.6 33.0 %all-to-all-done.3 = bf16[64,6,2048]{2,1,0:T(8,128)(2,1)S(1)} async-done(((bf16[64,6,2048]{2,1,0:T(8,128)(2,1)}), bf16[64,6,2048]{2,1,0:T(8,128)(2,1)S(1)}, u32[]{:S(2)}, u32[]{:S(2)}) %all-to-all-start.3) | async-done | bytes 1572896 | tf_op jit(solution)/shard_map/all_to_all | solution.py:105
  278.5 1.4 all_to_all.43
  280.0 3.2 convolution_add_fusion
  283.2 1.5 convert_element_type.67
  284.8 40.3 %reduce-scatter.5.cloned.1.call-done = f32[128,256]{1,0:T(8,128)} async-done(((f32[128,2048]{1,0:T(8,128)}), f32[128,256]{1,0:T(8,128)}) %reduce-scatter.5.cloned.1.call-update) | async-done | bytes 131088 | tf_op jit(solution)/shard_map/reduce_scatter | solution.py:123
  325.1 1.5 convert_element_type.76
  (59 shorter events, 12.1 us)
Async XLA Ops:
  7.2 112.4 %copy-start = (bf16[1,176,2048]{2,1,0:T(8,128)(2,1)S(1)}, bf16[1,176,2048]{2,1,0:T(8,128)(2,1)}, u32[]{:S(2)}) copy-start(bf16[1,176,2048]{2,1,0:T(8,128)(2,1)} %param.19) | copy-start | bytes 2162692
  41.1 14.0 %copy-start.15 = (f32[128,6]{0,1:T(8,128)S(1)}, f32[128,6]{0,1:T(8,128)}, u32[]{:S(2)}) copy-start(f32[128,6]{0,1:T(8,128)} %param.13) | copy-start | bytes 9220
  41.1 14.5 %copy-start.14 = (bf16[128,256]{1,0:T(8,128)(2,1)S(1)}, bf16[128,256]{1,0:T(8,128)(2,1)}, u32[]{:S(2)}) copy-start(bf16[128,256]{1,0:T(8,128)(2,1)} %param.11) | copy-start | bytes 196612
  41.1 63.5 %all-to-all-start = ((bf16[64,6,2048]{2,1,0:T(8,128)(2,1)}), bf16[64,6,2048]{2,1,0:T(8,128)(2,1)S(1)}, u32[]{:S(2)}, u32[]{:S(2)}) async-start(bf16[64,6,2048]{2,1,0:T(8,128)(2,1)} %all_to_all.32), calls=%async_computation | async-start | bytes 4194304 | tf_op jit(solution)/shard_map/all_to_all | solution.py:53
  81.1 0.8 copy-start.3
  104.6 1.3 copy-start.2
  105.9 57.2 %all-to-all-start.2 = ((bf16[64,6,2048]{2,1,0:T(8,128)(2,1)}), bf16[64,6,2048]{2,1,0:T(8,128)(2,1)}, u32[]{:S(2)}, u32[]{:S(2)}) async-start(bf16[64,6,2048]{2,1,0:T(8,128)(2,1)} %all_to_all.38), calls=%async_computation.3 | async-start | bytes 4194304 | tf_op jit(solution)/shard_map/all_to_all | solution.py:54
  116.3 1.9 copy-start.12
  118.1 2.0 copy-start.8
  118.8 0.7 copy-start.9
  163.1 57.1 %all-to-all-start.1 = ((bf16[64,6,2048]{2,1,0:T(8,128)(2,1)}), bf16[64,6,2048]{2,1,0:T(8,128)(2,1)S(1)}, u32[]{:S(2)}, u32[]{:S(2)}) async-start(bf16[64,6,2048]{2,1,0:T(8,128)(2,1)} %all_to_all.35), calls=%async_computation.1 | async-start | bytes 4194304 | tf_op jit(solution)/shard_map/all_to_all | solution.py:104
  174.4 2.3 copy-start.11
  174.4 2.3 copy-start.13
  220.2 1.3 copy-start.1
  221.5 57.1 %all-to-all-start.3 = ((bf16[64,6,2048]{2,1,0:T(8,128)(2,1)}), bf16[64,6,2048]{2,1,0:T(8,128)(2,1)S(1)}, u32[]{:S(2)}, u32[]{:S(2)}) async-start(bf16[64,6,2048]{2,1,0:T(8,128)(2,1)} %all_to_all.41), calls=%async_computation.4 | async-start | bytes 4194304 | tf_op jit(solution)/shard_map/all_to_all | solution.py:105
  229.0 54.2 %reduce-scatter.3.cloned.1.call-start = ((), (), s32[]{:S(2)}) async-start(), calls=%async_computation.6 | async-start | bytes 1179648 | tf_op jit(solution)/shard_map/reduce_scatter | solution.py:122
  229.2 3.1 copy-start.5
  230.8 1.5 copy-start.10
  237.4 3.9 %copy-start.4 = (bf16[128,2048]{1,0:T(8,128)(2,1)S(1)}, bf16[128,2048]{1,0:T(8,128)(2,1)}, u32[]{:S(2)}) copy-start(bf16[128,2048]{1,0:T(8,128)(2,1)} %copy-done.3) | copy-start | bytes 1572868
  241.3 83.8 %reduce-scatter.5.cloned.1.call-start = ((), (), s32[]{:S(2)}) async-start(), calls=%async_computation.7 | async-start | bytes 1179648 | tf_op jit(solution)/shard_map/reduce_scatter | solution.py:123
  241.4 1.6 copy-start.6
  241.4 2.8 copy-start.7
Sparse Core Ops, SparseCore 0:
  241.4 40.5 reduce-scatter.2
  284.8 40.1 reduce-scatter.4
where the time goes:
time: 335 us; the launch traced here: 333 us
  waiting for transfers between devices  170 us (51%)
  blocking collectives  52.6 us (16%)
  starting transfers between devices  37 us (11%)
  local copies, waits for them, and re-layouts  28.1 us (8%)
  matrix products  25.5 us (8%)
  between operations  14.4 us (4%)
  other arithmetic  6.19 us (2%)
    all_to_all x1, waiting for transfers between devices, on_device(): lax.all_to_all(g_slots, 'expert', split_axis=0, concat_axis=0, tiled=True)  41.4 us
    reduce_scatter x1, waiting for transfers between devices, on_device(): lax.psum_scatter(early_input, 'tensor', scatter_dimension=1, tiled=True)  40.3 us
    all_to_all x1, waiting for transfers between devices, on_device(): lax.all_to_all(value_part, 'expert', split_axis=0, concat_axis=0, tiled=T...  37.6 us
    all_to_all x1, waiting for transfers between devices, on_device(): lax.all_to_all(input_part, 'expert', split_axis=0, concat_axis=0, tiled=T...  33 us
    all_gather x1, blocking collectives, on_device(): lax.all_gather(tokens, 'tensor', axis=1, tiled=True)  27.1 us
    all_gather x1, blocking collectives, on_device(): lax.all_gather(cotangent, 'tensor', axis=1, tiled=True)  25.5 us
    all_to_all x1, waiting for transfers between devices, on_device(): lax.all_to_all(x_slots, 'expert', split_axis=0, concat_axis=0, tiled=True)  17.3 us
    all_to_all x1, starting transfers between devices, on_device(): lax.all_to_all(x_slots, 'expert', split_axis=0, concat_axis=0, tiled=True)  14 us
  transfers between devices with their start and end apart: 6, of which 5 were waited for; matrix products, arithmetic and copies ran while one was open for 8% of the time, Pallas kernels for 0%

commit v1 on v0

--- a/solution.py
+++ b/solution.py
@@ -2,6 +2,34 @@
 import jax.numpy as jnp
 from jax import lax
 from jax.sharding import PartitionSpec as P
+
+
+def edit_ladders(w_in, along_dim):
+    w_in = jnp.moveaxis(w_in, 0, along_dim)
+    known = w_in.shape
+    return w_in.reshape(
+        *known[:along_dim], known[along_dim] * known[along_dim + 1], *known[along_dim + 2 :]
+    )
+
+
+def answer_the_panel(load, mesh_ax, d_out):
+    nodes = jax.lax.axis_size(mesh_ax)
+    so_far_all = list(map(lambda s: (s, (s + 1) % nodes), range(nodes)))
+    right_arr, arr_next = ([], [])
+    sides = [(num, to_i) for to_i, num in so_far_all]
+    for jj in range(nodes - 1):
+        if jj % 2 == 0:
+            right_arr.append(
+                jax.lax.ppermute(right_arr[-1] if right_arr else load, mesh_ax, perm=so_far_all)
+            )
+        else:
+            arr_next.append(
+                jax.lax.ppermute(arr_next[-1] if arr_next else load, axis_name=mesh_ax, perm=sides)
+            )
+    lower = jnp.stack([*right_arr[::-1], load, *arr_next])
+    parts_out = jax.lax.axis_index(mesh_ax) - len(right_arr)
+    lower = lower[(jnp.arange(nodes) - parts_out) % nodes]
+    return edit_ladders(lower, d_out)
 
 
 def silu_parts(pre_act):
@@ -42,7 +70,7 @@
     slot_gate = jnp.sum(jnp.where(slot_match, gate_flat[None, :], 0.0), axis=1)
     gate_dispatch = dispatch.astype(jnp.float32) * slot_gate[:, None]
     x_full, c_full = (
-        lax.all_gather(tokens, "tensor", axis=1, tiled=True),
+        answer_the_panel(tokens, "tensor", 1),
         lax.all_gather(cotangent, "tensor", axis=1, tiled=True),
     )
     x_slots = jnp.dot(dispatch, x_full, preferred_element_type=jnp.float32).astype(jnp.bfloat16)

time: 335 us -> 345 us (1.030)
  blocking collectives: 52.6 us -> 26.9 us
  starting transfers between devices: 37 us -> 60.7 us
  waiting for transfers between devices: 170 us -> 180 us
    reduce_scatter x1, waiting for transfers between devices: 40.3 us -> 0.02 us  [on_device(): lax.psum_scatter(early_input, 'tensor', scatter_dimension=1, tiled=True)]
    reduce_scatter x1, waiting for transfers between devices: 0.02 us -> 40 us  [on_device(): lax.psum_scatter(early_value, 'tensor', scatter_dimension=1, tiled=True)]
    all_to_all x1, waiting for transfers between devices: 41.4 us -> 10.2 us  [on_device(): lax.all_to_all(g_slots, 'expert', split_axis=0, concat_axis=0, tiled=True)]
    all_to_all x1, waiting for transfers between devices: 17.3 us -> 48 us  [on_device(): lax.all_to_all(x_slots, 'expert', split_axis=0, concat_axis=0, tiled=True)]
    all_gather x1 -> x0, blocking collectives: 27.1 us -> none  [on_device(): lax.all_gather(tokens, 'tensor', axis=1, tiled=True)]
    ppermute x0 -> x7, starting transfers between devices: none -> 23.9 us  [the longest x3 15.4 us: answer_the_panel(): jax.lax.ppermute(arr_next[-1] if arr_next else load, axis_name=mesh_ax, p...]
    all_to_all x1, waiting for transfers between devices: 33 us -> 41.4 us  [on_device(): lax.all_to_all(input_part, 'expert', split_axis=0, concat_axis=0, tiled=T...]
    all_to_all x1, starting transfers between devices: 7.71 us -> 14 us  [on_device(): lax.all_to_all(g_slots, 'expert', split_axis=0, concat_axis=0, tiled=True)]
  transfers between devices with their start and end apart: 6 -> 13, of which waited for: 5 -> 9; matrix products, arithmetic and copies ran while one was open for 8% -> 8% of each run, Pallas kernels for 0% -> 0%
where the time goes in v1:
time: 345 us; the launch traced here: 343 us
  waiting for transfers between devices  180 us (52%)
  starting transfers between devices  60.7 us (18%)
  local copies, waits for them, and re-layouts  30.1 us (9%)
  blocking collectives  26.9 us (8%)
  matrix products  25 us (7%)
  between operations  14.5 us (4%)
  other arithmetic  6.14 us (2%)
    all_to_all x1, waiting for transfers between devices, on_device(): lax.all_to_all(x_slots, 'expert', split_axis=0, concat_axis=0, tiled=True)  48 us
    all_to_all x1, waiting for transfers between devices, on_device(): lax.all_to_all(input_part, 'expert', split_axis=0, concat_axis=0, tiled=T...  41.4 us
    reduce_scatter x1, waiting for transfers between devices, on_device(): lax.psum_scatter(early_value, 'tensor', scatter_dimension=1, tiled=True)  40 us
    all_to_all x1, waiting for transfers between devices, on_device(): lax.all_to_all(value_part, 'expert', split_axis=0, concat_axis=0, tiled=T...  34.7 us
    all_gather x1, blocking collectives, on_device(): lax.all_gather(cotangent, 'tensor', axis=1, tiled=True)  26.9 us
    ppermute x3, starting transfers between devices, answer_the_panel(): jax.lax.ppermute(arr_next[-1] if arr_next else load, axis_name=mesh_ax, p...  15.4 us
    all_to_all x1, starting transfers between devices, on_device(): lax.all_to_all(g_slots, 'expert', split_axis=0, concat_axis=0, tiled=True)  14 us
    all_to_all x1, waiting for transfers between devices, on_device(): lax.all_to_all(g_slots, 'expert', split_axis=0, concat_axis=0, tiled=True)  10.2 us
  transfers between devices with their start and end apart: 13, of which 9 were waited for; matrix products, arithmetic and copies ran while one was open for 8% of the time, Pallas kernels for 0%

profile of v1, /device:TPU:2, one launch (start us, length us, event | category | flops | bytes accessed | tf_op | source)
XLA Modules:
  0.0 343.2 jit_solution(1316483135756925290)
XLA Ops:
  9.1 1.8 reduce-window.6
  12.1 26.9 %all_gather.3 = bf16[128,2048]{1,0:T(8,128)(2,1)S(1)} all-gather(bf16[128,256]{1,0:T(8,128)(2,1)S(1)} %copy-done.15), channel_id=1, replica_groups=mesh['expert'=64,'tensor'=8] {'tensor'}, dimensions={1}, use_global_device_ids=true | all-gather | bytes 589824 | tf_op jit(solution)/shard_map/all_gather | solution.py:74
  40.4 1.6 all_to_all.38
  42.0 14.0 %all-to-all-start.2 = ((bf16[64,6,2048]{2,1,0:T(8,128)(2,1)}), bf16[64,6,2048]{2,1,0:T(8,128)(2,1)S(1)}, u32[]{:S(2)}, u32[]{:S(2)}) async-start(bf16[64,6,2048]{2,1,0:T(8,128)(2,1)} %all_to_all.38), calls=%async_computation.3 | async-start | bytes 4194304 | tf_op jit(solution)/shard_map/all_to_all | solution.py:82
  56.0 2.7 collective-permute-start
  58.8 4.6 %collective-permute-done = bf16[128,256]{1,0:T(8,128)(2,1)S(1)} collective-permute-done((bf16[128,256]{1,0:T(8,128)(2,1)S(1)}, bf16[128,256]{1,0:T(8,128)(2,1)S(1)}, u32[]{:S(2)}, u32[]{:S(2)}) %collective-permute-start) | collective-permute-done | bytes 65568 | tf_op jit(solution)/shard_map/ppermute | solution.py:23
  63.4 1.9 collective-permute-start.1
  65.3 5.1 %collective-permute-start.4 = (bf16[128,256]{1,0:T(8,128)(2,1)S(1)}, bf16[128,256]{1,0:T(8,128)(2,1)S(1)}, u32[]{:S(2)}, u32[]{:S(2)}) collective-permute-start(bf16[128,256]{1,0:T(8,128)(2,1)S(1)} %copy-done.16), channel_id=1, source_target_pairs={{1,0},{2,1},{3,2},{4,3},{5,4},{6,5},{7,6},{0,7},{9,8},{10,9},{11,1... | collective-permute-start | bytes 196616 | tf_op jit(solution)/shard_map/ppermute | solution.py:27
  70.8 1.9 collective-permute-start.2
  72.7 5.1 %collective-permute-start.5 = (bf16[128,256]{1,0:T(8,128)(2,1)S(1)}, bf16[128,256]{1,0:T(8,128)(2,1)S(1)}, u32[]{:S(2)}, u32[]{:S(2)}) collective-permute-start(bf16[128,256]{1,0:T(8,128)(2,1)S(1)} %collective-permute-done.4), channel_id=1, source_target_pairs={{1,0},{2,1},{3,2},{4,3},{5,4},{6,5},{7,6},{0,7},{9,8},{10,9},{11,1... | collective-permute-start | bytes 196616 | tf_op jit(solution)/shard_map/ppermute | solution.py:27
  78.1 1.9 collective-permute-start.3
  80.1 5.1 %collective-permute-start.6 = (bf16[128,256]{1,0:T(8,128)(2,1)S(1)}, bf16[128,256]{1,0:T(8,128)(2,1)S(1)}, u32[]{:S(2)}, u32[]{:S(2)}) collective-permute-start(bf16[128,256]{1,0:T(8,128)(2,1)S(1)} %collective-permute-done.5), channel_id=1, source_target_pairs={{1,0},{2,1},{3,2},{4,3},{5,4},{6,5},{7,6},{0,7},{9,8},{10,9},{11,1... | collective-permute-start | bytes 196616 | tf_op jit(solution)/shard_map/ppermute | solution.py:27
  90.0 1.8 convolution_convert_fusion.2
  91.7 3.7 %all_to_all.32 = bf16[64,6,2048]{2,1,0:T(8,128)(2,1)} reshape(bf16[384,2048]{1,0:T(8,128)(2,1)} %convolution_convert_fusion.2) | data formatting | bytes 3145728 | tf_op jit(solution)/shard_map/all_to_all | solution.py:81
  95.4 10.2 %all-to-all-done.2 = bf16[64,6,2048]{2,1,0:T(8,128)(2,1)S(1)} async-done(((bf16[64,6,2048]{2,1,0:T(8,128)(2,1)}), bf16[64,6,2048]{2,1,0:T(8,128)(2,1)S(1)}, u32[]{:S(2)}, u32[]{:S(2)}) %all-to-all-start.2) | async-done | bytes 1572896 | tf_op jit(solution)/shard_map/all_to_all | solution.py:82
  105.6 7.7 %all-to-all-start = ((bf16[64,6,2048]{2,1,0:T(8,128)(2,1)}), bf16[64,6,2048]{2,1,0:T(8,128)(2,1)}, u32[]{:S(2)}, u32[]{:S(2)}) async-start(bf16[64,6,2048]{2,1,0:T(8,128)(2,1)} %all_to_all.32), calls=%async_computation | async-start | bytes 4194304 | tf_op jit(solution)/shard_map/all_to_all | solution.py:81
  114.8 48.0 %all-to-all-done = bf16[64,6,2048]{2,1,0:T(8,128)(2,1)} async-done(((bf16[64,6,2048]{2,1,0:T(8,128)(2,1)}), bf16[64,6,2048]{2,1,0:T(8,128)(2,1)}, u32[]{:S(2)}, u32[]{:S(2)}) %all-to-all-start) | async-done | bytes 1572896 | tf_op jit(solution)/shard_map/all_to_all | solution.py:81
  162.7 2.6 all_to_all.34
  165.4 1.8 fusion.6
  171.0 1.6 all_to_all.41
  172.6 7.5 %all-to-all-start.3 = ((bf16[64,6,2048]{2,1,0:T(8,128)(2,1)}), bf16[64,6,2048]{2,1,0:T(8,128)(2,1)S(1)}, u32[]{:S(2)}, u32[]{:S(2)}) async-start(bf16[64,6,2048]{2,1,0:T(8,128)(2,1)} %all_to_all.41), calls=%async_computation.4 | async-start | bytes 4194304 | tf_op jit(solution)/shard_map/all_to_all | solution.py:133
  180.1 1.6 fusion.39
  181.7 2.8 convolution_convert_fusion
  184.6 3.7 %all_to_all.35 = bf16[64,6,2048]{2,1,0:T(8,128)(2,1)} reshape(bf16[384,2048]{1,0:T(8,128)(2,1)} %convolution_convert_fusion) | data formatting | bytes 3145728 | tf_op jit(solution)/shard_map/all_to_all | solution.py:132
  188.2 41.4 %all-to-all-done.3 = bf16[64,6,2048]{2,1,0:T(8,128)(2,1)S(1)} async-done(((bf16[64,6,2048]{2,1,0:T(8,128)(2,1)}), bf16[64,6,2048]{2,1,0:T(8,128)(2,1)S(1)}, u32[]{:S(2)}, u32[]{:S(2)}) %all-to-all-start.3) | async-done | bytes 1572896 | tf_op jit(solution)/shard_map/all_to_all | solution.py:133
  231.0 7.5 %all-to-all-start.1 = ((bf16[64,6,2048]{2,1,0:T(8,128)(2,1)}), bf16[64,6,2048]{2,1,0:T(8,128)(2,1)S(1)}, u32[]{:S(2)}, u32[]{:S(2)}) async-start(bf16[64,6,2048]{2,1,0:T(8,128)(2,1)} %all_to_all.35), calls=%async_computation.1 | async-start | bytes 4194304 | tf_op jit(solution)/shard_map/all_to_all | solution.py:132
  244.0 3.7 %all_to_all.43 = bf16[384,2048]{1,0:T(8,128)(2,1)} reshape(bf16[64,6,2048]{2,1,0:T(8,128)(2,1)} %copy-done.1) | data formatting | bytes 3145728 | tf_op jit(solution)/shard_map/all_to_all | solution.py:133
  247.7 3.3 convolution_add_fusion
  251.1 2.3 fusion.25
  253.3 34.7 %all-to-all-done.1 = bf16[64,6,2048]{2,1,0:T(8,128)(2,1)S(1)} async-done(((bf16[64,6,2048]{2,1,0:T(8,128)(2,1)}), bf16[64,6,2048]{2,1,0:T(8,128)(2,1)S(1)}, u32[]{:S(2)}, u32[]{:S(2)}) %all-to-all-start.1) | async-done | bytes 1572896 | tf_op jit(solution)/shard_map/all_to_all | solution.py:132
  289.5 3.8 %convolution_add_fusion.2 = f32[128,2048]{1,0:T(8,128)} fusion(f32[128,2048]{1,0:T(8,128)} %fusion.25, bf16[384,2048]{1,0:T(8,128)(2,1)} %all_to_all.37, f32[384]{0:T(512)S(1)} %select_reduce_fusion, pred[384,128]{1,0:T(8,128)(4,1)S(1)} %copy-done.9), kind=kOutput, calls=%fused_computation.7 | convolution fusion | flops 1208369152 | bytes 3720704 | tf_op jit(solution)/shard_map/st,sd->td/dot_general | solution.py:135
  294.8 40.0 %reduce-scatter.3.cloned.1.call-done = f32[128,256]{1,0:T(8,128)} async-done(((f32[128,2048]{1,0:T(8,128)}), f32[128,256]{1,0:T(8,128)}) %reduce-scatter.3.cloned.1.call-update) | async-done | bytes 131088 | tf_op jit(solution)/shard_map/reduce_scatter | solution.py:150
  (92 shorter events, 26.2 us)
Async XLA Ops:
  7.2 160.8 %copy-start = (bf16[1,176,2048]{2,1,0:T(8,128)(2,1)S(1)}, bf16[1,176,2048]{2,1,0:T(8,128)(2,1)}, u32[]{:S(2)}) copy-start(bf16[1,176,2048]{2,1,0:T(8,128)(2,1)} %param.19) | copy-start | bytes 2162692
  7.2 4.6 %copy-start.19 = (f32[128,6]{0,1:T(8,128)S(1)}, f32[128,6]{0,1:T(8,128)}, u32[]{:S(2)}) copy-start(f32[128,6]{0,1:T(8,128)} %param.13) | copy-start | bytes 9220
  7.2 4.9 %copy-start.15 = (bf16[128,256]{1,0:T(8,128)(2,1)S(1)}, bf16[128,256]{1,0:T(8,128)(2,1)}, u32[]{:S(2)}) copy-start(bf16[128,256]{1,0:T(8,128)(2,1)} %param.11) | copy-start | bytes 196612
  11.8 78.1 %copy-start.8 = (pred[384,128]{1,0:T(8,128)(4,1)}, pred[384,128]{1,0:T(8,128)(4,1)S(1)}, u32[]{:S(2)}) copy-start(pred[384,128]{1,0:T(8,128)(4,1)S(1)} %fusion.2) | copy-start | bytes 147460
  39.0 0.8 copy-start.2
  42.0 14.0 %copy-start.16 = (bf16[128,256]{1,0:T(8,128)(2,1)S(1)}, bf16[128,256]{1,0:T(8,128)(2,1)}, u32[]{:S(2)}) copy-start(bf16[128,256]{1,0:T(8,128)(2,1)} %param.10) | copy-start | bytes 196612
  42.0 63.6 %all-to-all-start.2 = ((bf16[64,6,2048]{2,1,0:T(8,128)(2,1)}), bf16[64,6,2048]{2,1,0:T(8,128)(2,1)S(1)}, u32[]{:S(2)}, u32[]{:S(2)}) async-start(bf16[64,6,2048]{2,1,0:T(8,128)(2,1)} %all_to_all.38), calls=%async_computation.3 | async-start | bytes 4194304 | tf_op jit(solution)/shard_map/all_to_all | solution.py:82
  56.0 7.4 %collective-permute-start = (bf16[128,256]{1,0:T(8,128)(2,1)S(1)}, bf16[128,256]{1,0:T(8,128)(2,1)S(1)}, u32[]{:S(2)}, u32[]{:S(2)}) collective-permute-start(bf16[128,256]{1,0:T(8,128)(2,1)S(1)} %copy-done.16), channel_id=1, source_target_pairs={{0,1},{1,2},{2,3},{3,4},{4,5},{5,6},{6,7},{7,0},{8,9},{9,10},{10,1... | collective-permute-start | bytes 196616 | tf_op jit(solution)/shard_map/ppermute | solution.py:23
  63.4 7.4 %collective-permute-start.1 = (bf16[128,256]{1,0:T(8,128)(2,1)S(1)}, bf16[128,256]{1,0:T(8,128)(2,1)S(1)}, u32[]{:S(2)}, u32[]{:S(2)}) collective-permute-start(bf16[128,256]{1,0:T(8,128)(2,1)S(1)} %collective-permute-done), channel_id=1, source_target_pairs={{0,1},{1,2},{2,3},{3,4},{4,5},{5,6},{6,7},{7,0},{8,9},{9,10},{10,1... | collective-permute-start | bytes 196616 | tf_op jit(solution)/shard_map/ppermute | solution.py:23
  65.3 7.4 %collective-permute-start.4 = (bf16[128,256]{1,0:T(8,128)(2,1)S(1)}, bf16[128,256]{1,0:T(8,128)(2,1)S(1)}, u32[]{:S(2)}, u32[]{:S(2)}) collective-permute-start(bf16[128,256]{1,0:T(8,128)(2,1)S(1)} %copy-done.16), channel_id=1, source_target_pairs={{1,0},{2,1},{3,2},{4,3},{5,4},{6,5},{7,6},{0,7},{9,8},{10,9},{11,1... | collective-permute-start | bytes 196616 | tf_op jit(solution)/shard_map/ppermute | solution.py:27
  70.8 14.5 %copy-start.18 = (bf16[128,256]{1,0:T(8,128)(2,1)}, bf16[128,256]{1,0:T(8,128)(2,1)S(1)}, u32[]{:S(2)}) copy-start(bf16[128,256]{1,0:T(8,128)(2,1)S(1)} %collective-permute-done.1) | copy-start | bytes 196612
  70.8 7.4 %collective-permute-start.2 = (bf16[128,256]{1,0:T(8,128)(2,1)S(1)}, bf16[128,256]{1,0:T(8,128)(2,1)S(1)}, u32[]{:S(2)}, u32[]{:S(2)}) collective-permute-start(bf16[128,256]{1,0:T(8,128)(2,1)S(1)} %collective-permute-done.1), channel_id=1, source_target_pairs={{0,1},{1,2},{2,3},{3,4},{4,5},{5,6},{6,7},{7,0},{8,9},{9,10},{10,1... | collective-permute-start | bytes 196616 | tf_op jit(solution)/shard_map/ppermute | solution.py:23
  72.7 12.5 %copy-start.17 = (bf16[128,256]{1,0:T(8,128)(2,1)}, bf16[128,256]{1,0:T(8,128)(2,1)S(1)}, u32[]{:S(2)}) copy-start(bf16[128,256]{1,0:T(8,128)(2,1)S(1)} %collective-permute-done.4) | copy-start | bytes 196612
  72.7 7.3 %collective-permute-start.5 = (bf16[128,256]{1,0:T(8,128)(2,1)S(1)}, bf16[128,256]{1,0:T(8,128)(2,1)S(1)}, u32[]{:S(2)}, u32[]{:S(2)}) collective-permute-start(bf16[128,256]{1,0:T(8,128)(2,1)S(1)} %collective-permute-done.4), channel_id=1, source_target_pairs={{1,0},{2,1},{3,2},{4,3},{5,4},{6,5},{7,6},{0,7},{9,8},{10,9},{11,1... | collective-permute-start | bytes 196616 | tf_op jit(solution)/shard_map/ppermute | solution.py:27
  78.1 7.4 %collective-permute-start.3 = (bf16[128,256]{1,0:T(8,128)(2,1)S(1)}, bf16[128,256]{1,0:T(8,128)(2,1)S(1)}, u32[]{:S(2)}, u32[]{:S(2)}) collective-permute-start(bf16[128,256]{1,0:T(8,128)(2,1)S(1)} %collective-permute-done.2), channel_id=1, source_target_pairs={{0,1},{1,2},{2,3},{3,4},{4,5},{5,6},{6,7},{7,0},{8,9},{9,10},{10,1... | collective-permute-start | bytes 196616 | tf_op jit(solution)/shard_map/ppermute | solution.py:23
  80.1 7.2 %collective-permute-start.6 = (bf16[128,256]{1,0:T(8,128)(2,1)S(1)}, bf16[128,256]{1,0:T(8,128)(2,1)S(1)}, u32[]{:S(2)}, u32[]{:S(2)}) collective-permute-start(bf16[128,256]{1,0:T(8,128)(2,1)S(1)} %collective-permute-done.5), channel_id=1, source_target_pairs={{1,0},{2,1},{3,2},{4,3},{5,4},{6,5},{7,6},{0,7},{9,8},{10,9},{11,1... | collective-permute-start | bytes 196616 | tf_op jit(solution)/shard_map/ppermute | solution.py:27
  105.6 57.2 %all-to-all-start = ((bf16[64,6,2048]{2,1,0:T(8,128)(2,1)}), bf16[64,6,2048]{2,1,0:T(8,128)(2,1)}, u32[]{:S(2)}, u32[]{:S(2)}) async-start(bf16[64,6,2048]{2,1,0:T(8,128)(2,1)} %all_to_all.32), calls=%async_computation | async-start | bytes 4194304 | tf_op jit(solution)/shard_map/all_to_all | solution.py:81
  165.4 1.9 copy-start.14
  167.2 2.2 copy-start.10
  167.2 1.5 copy-start.6
  168.7 0.7 copy-start.11
  168.7 1.2 copy-start.13
  172.6 57.1 %all-to-all-start.3 = ((bf16[64,6,2048]{2,1,0:T(8,128)(2,1)}), bf16[64,6,2048]{2,1,0:T(8,128)(2,1)S(1)}, u32[]{:S(2)}, u32[]{:S(2)}) async-start(bf16[64,6,2048]{2,1,0:T(8,128)(2,1)} %all_to_all.41), calls=%async_computation.4 | async-start | bytes 4194304 | tf_op jit(solution)/shard_map/all_to_all | solution.py:133
  229.6 1.3 copy-start.1
  231.0 57.1 %all-to-all-start.1 = ((bf16[64,6,2048]{2,1,0:T(8,128)(2,1)}), bf16[64,6,2048]{2,1,0:T(8,128)(2,1)S(1)}, u32[]{:S(2)}, u32[]{:S(2)}) async-start(bf16[64,6,2048]{2,1,0:T(8,128)(2,1)} %all_to_all.35), calls=%async_computation.1 | async-start | bytes 4194304 | tf_op jit(solution)/shard_map/all_to_all | solution.py:132
  238.5 54.8 %reduce-scatter.5.cloned.1.call-start = ((), (), s32[]{:S(2)}) async-start(), calls=%async_computation.7 | async-start | bytes 1179648 | tf_op jit(solution)/shard_map/reduce_scatter | solution.py:151
  238.5 3.7 %copy-start.3 = (bf16[176,2048]{1,0:T(8,128)(2,1)S(1)}, bf16[176,2048]{1,0:T(8,128)(2,1)}, u32[]{:S(2)}) copy-start(bf16[176,2048]{1,0:T(8,128)(2,1)} %param.14) | copy-start | bytes 2162692
  240.1 2.5 copy-start.7
  240.1 2.5 copy-start.4
  247.7 3.3 copy-start.5
  251.0 83.8 %reduce-scatter.3.cloned.1.call-start = ((), (), s32[]{:S(2)}) async-start(), calls=%async_computation.6 | async-start | bytes 1179648 | tf_op jit(solution)/shard_map/reduce_scatter | solution.py:150
  253.3 36.2 %copy-start.9 = (pred[384,128]{1,0:T(8,128)(4,1)S(1)}, pred[384,128]{1,0:T(8,128)(4,1)}, u32[]{:S(2)}) copy-start(pred[384,128]{1,0:T(8,128)(4,1)} %copy-done.8) | copy-start | bytes 147460
  (1 other events, 0.6 us)
Sparse Core Ops, SparseCore 0:
  251.1 40.6 reduce-scatter.4
  294.6 40.1 reduce-scatter.2
